TPU v7x, 256 devices: a whole 4x4x8 slice. The times are simulated.
256 devices in a mesh: dp: 32 (over z, y), tensor: 8 (over x, core).
Axes of the slice: x: 4, y: 4, z: 8, core: 2. Of those that a mesh axis runs over, the one named last changes fastest.
Arguments:
- inputs: bfloat16 [32768, 8192], P(('dp', 'tensor')), may hold values from -6 to 6
- out_grads: bfloat16 [32768, 2048], P('dp', 'tensor'), may hold values from -0.1875 to 0.1875
- error_in: bfloat16 [32, 8192, 2048], P('dp', None, 'tensor'), may hold values from -6 to 6
- basis_in: float32 [2048, 128], P('tensor'), may hold values from -6 to 6
Outputs:
- rebuilt: bfloat16 [8192, 2048], P('dp', 'tensor')
- error_out: bfloat16 [32, 8192, 2048], P('dp', None, 'tensor')
- basis_out: float32 [2048, 128], P('tensor')
All inputs are finite; a program needn't handle non-finite values.
Results may differ from a plain program's by a relative error of at most 0.0024.
Values may be sent and summed in bfloat16 or wider, within the bound.
A program may use at most 128 MiB of HBM per device.

v0:
```python
import jax
import jax.numpy as jnp
from jax import lax
from jax.sharding import PartitionSpec as P

highest = lax.Precision.HIGHEST


def right_solve(lower, values):
    return lax.linalg.triangular_solve(lower, values, left_side=False, lower=True, transpose_a=True)


def inner_rows(left, right):
    return lax.dot_general(
        left, right, (((0,), (0,)), ((), ())), precision=highest, preferred_element_type=jnp.float32
    )


def shards(inputs, out_grads, error_in, basis_in):
    replicas = lax.axis_size("dp")
    factor = 1.0 / replicas
    width = inputs.shape[1]
    gradient = lax.dot_general(
        lax.all_gather(inputs, "tensor", axis=0, tiled=True),
        out_grads,
        (((0,), (0,)), ((), ())),
        preferred_element_type=jnp.float32,
    )
    merged = gradient + error_in[0].astype(jnp.float32)
    partial_low = jnp.dot(merged, basis_in, precision=highest, preferred_element_type=jnp.float32)
    low_rank = lax.psum(partial_low, ("dp", "tensor")) * factor
    gram = inner_rows(low_rank, low_rank)
    lower = jnp.linalg.cholesky(gram)
    ortho = right_solve(lower, low_rank)
    basis = lax.psum(inner_rows(merged, ortho), "dp") * factor
    rebuilt_full = jnp.dot(ortho, basis.T, precision=highest, preferred_element_type=jnp.float32)
    error_out = (merged - rebuilt_full).astype(jnp.bfloat16)[None]
    share = width // replicas
    own_start = lax.axis_index("dp") * share
    own_rows = lax.dynamic_slice_in_dim(rebuilt_full, own_start, share, 0)
    return (own_rows.astype(jnp.bfloat16), error_out, basis)


def solution(mesh):
    placed = (
        P(("dp", "tensor"), None),
        P("dp", "tensor"),
        P("dp", None, "tensor"),
        P("tensor", None),
    )
    return jax.shard_map(
        shards,
        mesh=mesh,
        in_specs=placed,
        out_specs=(P("dp", "tensor"), P("dp", None, "tensor"), P("tensor", None)),
        check_vma=False,
    )
```

profile of v0, /device:TPU:2, one launch (start us, length us, event | category | flops | bytes accessed | tf_op | source)
XLA Modules:
  0.0 619.4 jit_solution(16607930259233007712)
XLA Ops:
  7.2 0.0 all-gather.2.cloned.1.call-start
  7.2 0.7 all-gather.2.cloned.1.call-update
  7.9 0.0 all-reduce.3.cloned.1.call-start
  8.0 92.0 %all-gather.2.cloned.1.call-done = bf16[1024,8192]{1,0:T(8,128)(2,1)} async-done(((bf16[128,8192]{1,0:T(8,128)(2,1)}), bf16[1024,8192]{1,0:T(8,128)(2,1)}) %all-gather.2.cloned.1.call-update) | async-done | bytes 16777232 | tf_op jit(solution)/shard_map/all_gather | solution.py:24
  100.0 12.2 %convolution_add_fusion = f32[8192,256]{1,0:T(8,128)S(1)} fusion(bf16[1024,8192]{1,0:T(8,128)(2,1)} %all-gather.2.cloned.1.call-done, bf16[1024,256]{1,0:T(8,128)(2,1)S(1)} %copy-done, bf16[1,8192,256]{2,1,0:T(8,128)(2,1)} %param.6), kind=kOutput, calls=%fused_computation | convolution fusion | flops 4299161600 | bytes 29884416 | tf_op jit(solution)/shard_map/dot_general | solution.py:23
  112.2 3.2 copy-done.1
  115.4 8.2 %fusion.12 = f32[8192,128]{1,0:T(8,128)} fusion(f32[8192,256]{1,0:T(8,128)S(1)} %convolution_add_fusion, f32[256,128]{1,0:T(8,128)S(1)} %copy-done.4), kind=kOutput, calls=%fused_computation.22 | convolution fusion | flops 3221225472 | bytes 12713984 | tf_op jit(solution)/shard_map/dot_general | solution.py:30
  123.6 0.0 all-reduce.3.cloned.1.call-update
  123.6 0.5 all-reduce.5.cloned.1.call-start
  124.1 269.3 %all-reduce.3.cloned.1.call-done = f32[8192,128]{1,0:T(8,128)} async-done(((f32[8192,128]{1,0:T(8,128)}), f32[8192,128]{1,0:T(8,128)}) %all-reduce.3.cloned.1.call-update) | async-done | bytes 4194320 | tf_op jit(solution)/shard_map/psum | solution.py:31
  393.5 10.5 %fusion.3 = f32[128,128]{1,0:T(8,128)S(1)} fusion(f32[8192,128]{1,0:T(8,128)} %all-reduce.3.cloned.1.call-done), kind=kOutput, calls=%fused_computation.5 | convolution fusion | flops 1611661312 | bytes 4259840 | tf_op jit(solution)/shard_map/dot_general | solution.py:14
  404.0 0.1 copy.7
  404.1 11.7 %cholesky.16 = f32[128,128]{1,0:T(8,128)S(1)} custom-call(f32[128,128]{1,0:T(8,128)S(1)} %fusion.9), custom_call_target="Cholesky" | custom-call | tf_op jit(solution)/shard_map/jit(cholesky)/cholesky | solution.py:33
  415.8 0.6 compare_reduce_fusion
  416.5 0.7 fusion.7
  417.1 9.9 %custom-call.6 = f32[1,128,128]{1,2,0:T(8,128)S(1)} custom-call(f32[1,128,128]{2,1,0:T(8,128)S(1)} %fusion.7), custom_call_target="InvertDiagBlocksLowerTriangular" | custom-call | tf_op jit(solution)/shard_map/triangular_solve | solution.py:10
  427.1 5.2 fusion.1
  432.3 2.0 copy-done.2
  434.3 16.3 %fusion.13 = f32[256,128]{1,0:T(8,128)} fusion(f32[8192,256]{1,0:T(8,128)} %copy-done.1, f32[8192,128]{1,0:T(8,128)S(1)} %fusion.1), kind=kOutput, calls=%fused_computation.23 | convolution fusion | flops 3221225472 | bytes 12713984 | tf_op jit(solution)/shard_map/dot_general | solution.py:14
  450.6 139.6 %all-reduce.5.cloned.1.call-done = f32[256,128]{1,0:T(8,128)} async-done(((f32[256,128]{1,0:T(8,128)}), f32[256,128]{1,0:T(8,128)}) %all-reduce.5.cloned.1.call-update) | async-done | bytes 131088 | tf_op jit(solution)/shard_map/psum | solution.py:35
  590.3 0.9 broadcast_multiply_fusion
  591.2 10.6 %fusion.14 = f32[8192,256]{1,0:T(8,128)} fusion(f32[8192,128]{1,0:T(8,128)} %copy-done.2, f32[256,128]{1,0:T(8,128)S(1)} %broadcast_multiply_fusion), kind=kOutput, calls=%fused_computation.24 | convolution fusion | flops 3221225472 | bytes 12713984 | tf_op jit(solution)/shard_map/dot_general | solution.py:36
  601.8 9.2 %fusion = bf16[1,8192,256]{2,1,0:T(8,128)(2,1)} fusion(f32[8192,256]{1,0:T(8,128)} %copy-done.1, f32[8192,256]{1,0:T(8,128)} %fusion.14), kind=kLoop, calls=%fused_computation.2 | loop fusion | flops 4194304 | bytes 20971520 | tf_op jit(solution)/shard_map/broadcast_in_dim | solution.py:37
  611.0 1.6 dynamic-slice_convert_fusion
  (11 shorter events, 0.1 us)
Async XLA Ops:
  7.2 92.8 %copy-start = (bf16[1024,256]{1,0:T(8,128)(2,1)S(1)}, bf16[1024,256]{1,0:T(8,128)(2,1)}, u32[]{:S(2)}) copy-start(bf16[1024,256]{1,0:T(8,128)(2,1)} %param.5) | copy-start | bytes 1572868
  7.2 92.8 %all-gather.2.cloned.1.call-start = ((), (), s32[]{:S(2)}) async-start(), calls=%async_computation | async-start | bytes 18874368 | tf_op jit(solution)/shard_map/all_gather | solution.py:24
  7.9 107.5 %copy-start.4 = (f32[256,128]{1,0:T(8,128)S(1)}, f32[256,128]{1,0:T(8,128)}, u32[]{:S(2)}) copy-start(f32[256,128]{1,0:T(8,128)} %param.7) | copy-start | bytes 393220
  7.9 385.5 %all-reduce.3.cloned.1.call-start = ((), (), s32[]{:S(2)}) async-start(), calls=%async_computation.1 | async-start | bytes 8388608 | tf_op jit(solution)/shard_map/psum | solution.py:31
  112.2 3.2 copy-start.1
  123.6 466.6 %all-reduce.5.cloned.1.call-start = ((), (), s32[]{:S(2)}) async-start(), calls=%async_computation.2 | async-start | bytes 262144 | tf_op jit(solution)/shard_map/psum | solution.py:35
  432.3 2.0 copy-start.2
  591.2 10.6 %copy-start.3 = (f32[256,128]{1,0:T(8,128)}, f32[256,128]{1,0:T(8,128)S(1)}, u32[]{:S(2)}) copy-start(f32[256,128]{1,0:T(8,128)S(1)} %broadcast_multiply_fusion) | copy-start | bytes 393220
Sparse Core Ops, SparseCore 0:
  9.9 90.0 all-gather.1
  123.8 269.6 all-reduce.2
  450.7 139.4 all-reduce.4
where the time goes:
time: 626 us; the launch traced here: 619 us
  waiting for transfers between devices  502 us (80%)
  matrix products  63 us (10%)
  other arithmetic  33.2 us (5%)
  between operations  14.1 us (2%)
  local copies, waits for them, and re-layouts  6.95 us (1%)
    psum x1, waiting for transfers between devices, shards(): low_rank = lax.psum(partial_low, ('dp', 'tensor')) * factor  269 us
    psum x1, waiting for transfers between devices, shards(): basis = lax.psum(inner_rows(merged, ortho), 'dp') * factor  140 us
    all_gather x1, waiting for transfers between devices, shards(): lax.all_gather(inputs, 'tensor', axis=0, tiled=True)  92 us
    dot_general x2, matrix products, inner_rows(): lax.dot_general(left, right, (((0,), (0,)), ((), ())), precision=highest,...  26.8 us
  transfers between devices with their start and end apart: 3, of which 3 were waited for; matrix products, arithmetic and copies ran while one was open for 0% of the time, Pallas kernels for 0%

commit v1 on v0

v1 whole, which is shorter than its diff:
```python
import functools

import jax
import jax.numpy as jnp
from jax import lax
from jax.experimental import pallas as pl
from jax.experimental.pallas import tpu as pltpu
from jax.sharding import PartitionSpec as P

NX = 4
NY = 4
RANK = 128
NCH = 4
XCH = 8
f32, bf16 = jnp.float32, jnp.bfloat16
MESH = pl.DeviceIdType.MESH
OVER_ROWS = (((0,), (0,)), ((), ()))


def split(value):
    high = value.astype(bf16)
    return high, (value - high.astype(f32)).astype(bf16)


def split_columns(value):
    return jnp.concatenate(split(value), axis=1)


def rows_dot(left, right, **kw):
    return lax.dot_general(left, right, OVER_ROWS, preferred_element_type=f32, **kw)


def dot(left, right, **kw):
    return jnp.dot(left, right, preferred_element_type=f32, **kw)


def exchange(
    nz, scale,
    x_hbm, g_hbm, e_hbm, basis,
    merged_hbm, lr_hbm, wt_ref, bt_ref,
    xg, g, e, p, d2d, yb, zb, xb, lr, merged,
    gb, gbd, gbx, bhl, gbhl,
    yt, yz, yy, yr, gram, aug,
    local, gb_s, gb_r, x_s, x_r, f_s, f_r, sib_s, sib_r,
    d_s, d_r, y_s, y_r, z_s, z_r, xx_s, xx_r,
    za_s, za_r, ya_s, ya_r, da_s, da_r,
    q_s, q_r, out_sem,
):
    width = x_hbm.shape[1]
    tok = x_hbm.shape[0]
    cols = e.shape[1]
    half = width // 2
    hc = half // NCH
    ybl = hc // NY
    zbl = ybl // nz
    cw = width // XCH
    dp = lax.axis_index("dp")
    t = lax.axis_index("tensor")
    z, y = dp // NY, dp % NY
    x, c = t // 2, t % 2
    sib = (dp, x * 2 + (1 - c))

    def at_x(o):
        return lax.rem(x + o + NX, NX)

    def to_x(o):
        return (dp, at_x(o) * 2 + c)

    def at_y(o):
        return lax.rem(y + o, NY)

    def to_y(o):
        return (z * NY + at_y(o), t)

    def at_z(o):
        return lax.rem(z + o, nz)

    def to_z(o):
        return (at_z(o) * NY + y, t)

    sent = []

    def send(src, dst, send_sem, recv_sem, device):
        copy = pltpu.make_async_remote_copy(
            src_ref=src, dst_ref=dst, send_sem=send_sem, recv_sem=recv_sem,
            device_id=device, device_id_type=MESH,
        )
        copy.start()
        sent.append(copy)
        return copy

    load_g = pltpu.make_async_copy(g_hbm, g, local.at[0])
    load_x = pltpu.make_async_copy(x_hbm, xg.at[t], local.at[1])
    load_e = pltpu.make_async_copy(e_hbm, e, local.at[2])
    load_g.start()
    load_x.start()
    load_e.start()

    barrier = pltpu.get_barrier_semaphore()
    partners = [sib] + [to_x(o) for o in range(1, NX)] + [to_y(o) for o in range(1, NY)] + [to_z(o) for o in range(1, nz)]
    for device in partners:
        pl.semaphore_signal(barrier, inc=1, device_id=device, device_id_type=MESH)

    bhl[...] = split_columns(basis[...])
    load_g.wait()
    for block in range(2 * NX):
        product = dot(g[block * tok:(block + 1) * tok, :], bhl[...])
        gb[block % 2, block // 2] = product[:, :RANK] + product[:, RANK:]
    pl.semaphore_wait(barrier, len(partners))
    gb_copy = send(gb.at[1 - c], gbd, gb_s.at[0], gb_r.at[0], sib)
    load_x.wait()
    gb_copy.wait_recv()
    gb[c] = gb[c] + gbd[...]
    gb_copies = [
        send(gb.at[c, at_x(o)], gbx.at[o - 1], gb_s.at[o], gb_r.at[o], to_x(o)) for o in range(1, NX)
    ]

    def chunk_of(shard, j):
        return xg.at[shard, :, pl.ds(j * cw, cw)]

    ring = []
    for j in range(XCH):
        ring.append([
            send(chunk_of(t, j), chunk_of(t, j), x_s.at[j, i], x_r.at[j, i], to_x(o))
            for i, o in enumerate((1, -1))
        ])
    own_sib = send(xg.at[t], xg.at[t], sib_s.at[XCH, 0], sib_r.at[XCH, 0], sib)

    far = [None] * XCH
    to_sib = [[] for _ in range(XCH)]

    def near(j):
        ring[j][0].wait_recv()
        ring[j][1].wait_recv()
        left = chunk_of(at_x(-1) * 2 + c, j)
        right = chunk_of(at_x(1) * 2 + c, j)
        if j % 2 == 0:
            far[j] = send(left, left, f_s.at[j], f_r.at[j], to_x(1))
        else:
            far[j] = send(right, right, f_s.at[j], f_r.at[j], to_x(-1))
        to_sib[j].append(send(left, left, sib_s.at[j, 0], sib_r.at[j, 0], sib))
        to_sib[j].append(send(right, right, sib_s.at[j, 1], sib_r.at[j, 1], sib))

    def distant(j):
        far[j].wait_recv()
        block = chunk_of(at_x(2) * 2 + c, j)
        to_sib[j].append(send(block, block, sib_s.at[j, 2], sib_r.at[j, 2], sib))

    merged_copies = []

    def multiply(j):
        if j == 0:
            own_sib.wait_recv()
        for copy in to_sib[j]:
            copy.wait_recv()
        tile = min(256, cw)

        @pl.loop(0, cw // tile)
        def _(i):
            row = pl.multiple_of(j * cw + i * tile, tile)
            block = xg[:, :, pl.ds(row, tile)].reshape(2 * NX * tok, tile)
            merged[pl.ds(row, tile), :] = rows_dot(block, g[...]) + e[pl.ds(row, tile), :].astype(f32)

        copy = pltpu.make_async_copy(
            merged.at[pl.ds(j * cw, cw)], merged_hbm.at[pl.ds(j * cw, cw)], out_sem.at[j])
        copy.start()
        merged_copies.append(copy)

    for copy in gb_copies:
        copy.wait_recv()
    gbhl[...] = split_columns(gb[c, x] + gbx[0] + gbx[1] + gbx[2])
    load_e.wait()

    def partial(h, k):
        tile = min(512, hc)

        @pl.loop(0, hc // tile)
        def _(i):
            at = pl.multiple_of(k * hc + i * tile, tile)
            row = pl.multiple_of(h * half + at, tile)
            total = rows_dot(xg[t, :, pl.ds(row, tile)], gbhl[...]) + dot(e[pl.ds(row, tile), :], bhl[...])
            p[h, pl.ds(at, tile), :] = total[:, :RANK] + total[:, RANK:]

    y_copies, z_copies, x_copies = {}, {}, {}
    za_copies, ya_copies, da_copies = {}, {}, {}
    for k in range(NCH):
        partial(1 - c, k)
        rows = pl.ds(k * hc, hc)
        d_copy = send(p.at[1 - c, rows], d2d.at[rows], d_s.at[k], d_r.at[k], sib)
        partial(c, k)
        d_copy.wait_recv()
        p[c, rows, :] = p[c, rows, :] + d2d[rows, :]
        y_copies[k] = [
            send(p.at[c, pl.ds(k * hc + at_y(o) * ybl, ybl)], yb.at[k, o - 1], y_s.at[k, o - 1], y_r.at[k, o - 1], to_y(o))
            for o in range(1, NY)
        ]

    def own_y(k):
        return pl.ds(pl.multiple_of(k * hc + y * ybl, ybl), ybl)

    def own_z(k):
        return pl.ds(pl.multiple_of(k * hc + y * ybl + z * zbl, zbl), zbl)

    def stage_y(k):
        for copy in y_copies[k]:
            copy.wait_recv()
        total = p[c, own_y(k), :]
        for i in range(NY - 1):
            total = total + yb[k, i]
        p[c, own_y(k), :] = total
        z_copies[k] = [
            send(p.at[c, pl.ds(pl.multiple_of(k * hc + y * ybl + at_z(o) * zbl, zbl), zbl)], zb.at[k, o - 1],
                 z_s.at[k, o - 1], z_r.at[k, o - 1], to_z(o))
            for o in range(1, nz)
        ]

    def stage_z(k):
        for copy in z_copies[k]:
            copy.wait_recv()
        total = p[c, own_z(k), :]
        for i in range(nz - 1):
            total = total + zb[k, i]
        xb[k, x] = total
        x_copies[k] = [
            send(xb.at[k, x], xb.at[k, x], xx_s.at[k, o - 1], xx_r.at[k, o - 1], to_x(o)) for o in range(1, NX)
        ]

    def stage_x(k):
        for copy in x_copies[k]:
            copy.wait_recv()
        total = xb[k, 0]
        for i in range(1, NX):
            total = total + xb[k, i]
        lr[c, own_z(k), :] = split_columns(total * scale)
        block = lr.at[c, own_z(k)]
        za_copies[k] = [
            send(block, block, za_s.at[k, o - 1], za_r.at[k, o - 1], to_z(o)) for o in range(1, nz)
        ]

    def gather_z(k):
        for copy in za_copies[k]:
            copy.wait_recv()
        block = lr.at[c, own_y(k)]
        ya_copies[k] = [
            send(block, block, ya_s.at[k, o - 1], ya_r.at[k, o - 1], to_y(o)) for o in range(1, NY)
        ]

    def gather_y(k):
        for copy in ya_copies[k]:
            copy.wait_recv()
        block = lr.at[c, pl.ds(k * hc, hc)]
        da_copies[k] = send(block, block, da_s.at[k], da_r.at[k], sib)

    lr_copies = []

    def gather_core(k):
        da_copies[k].wait_recv()
        for h in range(2):
            copy = pltpu.make_async_copy(
                lr.at[h, pl.ds(k * hc, hc)], lr_hbm.at[pl.ds(h * half + k * hc, hc)], out_sem.at[XCH + 2 * k + h])
            copy.start()
            lr_copies.append(copy)

    def right(h, k):
        tile = min(512, hc)

        @pl.loop(0, hc // tile)
        def _(i):
            at = pl.multiple_of(k * hc + i * tile, tile)
            pair = lr[h, pl.ds(at, tile), :]
            high, low = split(merged[pl.ds(pl.multiple_of(h * half + at, tile), tile), :])
            both = rows_dot(pair, high)
            yt[...] += both[:RANK] + both[RANK:] + rows_dot(pair[:, :RANK], low)
            square = rows_dot(pair, pair)
            gram[...] += (square[:RANK, :RANK] + square[RANK:, RANK:]) + (square[:RANK, RANK:] + square[RANK:, :RANK])

    yt[...] = jnp.zeros_like(yt)
    gram[...] = jnp.zeros_like(gram)
    stages = (stage_y, stage_z, stage_x, gather_z, gather_y, gather_core)
    for s in range(NCH + len(stages) - 1):
        for lag, stage in enumerate(stages):
            if 0 <= s - lag < NCH:
                stage(s - lag)
        if s < XCH:
            near(s)
    for j in range(XCH):
        distant(j)
    for j in range(XCH):
        multiply(j)
    for h in range(2):
        for k in range(NCH):
            right(h, k)

    lane = lax.broadcasted_iota(jnp.int32, (RANK, 2 * RANK), 1)
    sub = lax.broadcasted_iota(jnp.int32, (RANK, 2 * RANK), 0)
    aug[:, :RANK] = gram[...]
    aug[:, RANK:] = jnp.where(
        lax.broadcasted_iota(jnp.int32, (RANK, RANK), 0) == lax.broadcasted_iota(jnp.int32, (RANK, RANK), 1), 1.0, 0.0)

    def eliminate(first, last):
        @pl.loop(first, last)
        def _(j):
            row = aug[pl.ds(j, 1), :]
            pivot = jnp.sum(jnp.where(lane[:1] == j, row, 0.0), axis=1, keepdims=True)
            column = jnp.sum(jnp.where(lane == j, aug[...], 0.0), axis=1, keepdims=True)
            factor = jnp.where(sub[:, :1] > j, column / pivot, 0.0)
            aug[...] = aug[...] - factor * row

    part = RANK // nz
    own = pl.ds(pl.multiple_of(z * part, part), part)
    cuts = (0, RANK // 3, 2 * RANK // 3, RANK)
    copies = [
        send(yt.at[pl.ds(pl.multiple_of(at_z(o) * part, part), part)], yz.at[o - 1], q_s.at[0, o - 1], q_r.at[0, o - 1], to_z(o))
        for o in range(1, nz)
    ]
    eliminate(cuts[0], cuts[1])
    for copy in copies:
        copy.wait_recv()
    total = yt[own, :]
    for i in range(nz - 1):
        total = total + yz[i]
    yy[y] = total
    copies = [send(yy.at[y], yy.at[y], q_s.at[1, o - 1], q_r.at[1, o - 1], to_y(o)) for o in range(1, NY)]
    eliminate(cuts[1], cuts[2])
    for copy in copies:
        copy.wait_recv()
    total = yy[0]
    for i in range(1, NY):
        total = total + yy[i]
    yr[own, :] = total * scale
    copies = [send(yr.at[own], yr.at[own], q_s.at[2, o - 1], q_r.at[2, o - 1], to_z(o)) for o in range(1, nz)]
    eliminate(cuts[2], cuts[3])
    pivots = jnp.sum(jnp.where(lane == sub, aug[...], 0.0), axis=1, keepdims=True)
    inverse = aug[:, RANK:] / jnp.sqrt(pivots)
    for copy in copies:
        copy.wait_recv()
    bt = dot(inverse, yr[...], precision=lax.Precision.HIGHEST)
    bt_ref[...] = bt
    wt_ref[...] = rows_dot(inverse, bt, precision=lax.Precision.HIGHEST)
    for copy in sent:
        copy.wait_send()
    for copy in merged_copies + lr_copies:
        copy.wait()


def finish(index, merged, lr, lr_own, wt, bt, rebuilt_ref, error_ref, basis_ref):
    high, low = split(wt[...])
    twice = jnp.concatenate([high, high], axis=0)

    def rebuild(pair):
        return dot(pair, twice) + dot(pair[:, :RANK], low)

    error_ref[0] = (merged[...] - rebuild(lr[...])).astype(bf16)

    @pl.when(pl.program_id(0) == 0)
    def _():
        rebuilt_ref[...] = rebuild(lr_own[...]).astype(bf16)
        basis_ref[...] = bt[...].T


def shards(inputs, out_grads, error_in, basis_in):
    replicas = lax.axis_size("dp")
    nz = replicas // NY
    tok, width = inputs.shape
    tokens, cols = out_grads.shape
    half = width // 2
    hc = half // NCH
    ybl = hc // NY
    zbl = ybl // nz
    scratch = [
        ((2 * NX, tok, width), bf16),
        ((tokens, cols), bf16),
        ((width, cols), bf16),
        ((2, half, RANK), f32),
        ((half, RANK), f32),
        ((NCH, NY - 1, ybl, RANK), f32),
        ((NCH, nz - 1, zbl, RANK), f32),
        ((NCH, NX, zbl, RANK), f32),
        ((2, half, 2 * RANK), bf16),
        ((width, cols), f32),
        ((2, NX, tok, RANK), f32),
        ((NX, tok, RANK), f32),
        ((NX - 1, tok, RANK), f32),
        ((cols, 2 * RANK), bf16),
        ((tok, 2 * RANK), bf16),
        ((RANK, cols), f32),
        ((nz - 1, RANK // nz, cols), f32),
        ((NY, RANK // nz, cols), f32),
        ((RANK, cols), f32),
        ((RANK, RANK), f32),
        ((RANK, 2 * RANK), f32),
    ]
    sems = [
        (3,), (NX,), (NX,), (XCH, 2), (XCH, 2), (XCH,), (XCH,), (XCH + 1, 3), (XCH + 1, 3),
        (NCH,), (NCH,), (NCH, NY - 1), (NCH, NY - 1), (NCH, nz - 1), (NCH, nz - 1), (NCH, NX - 1), (NCH, NX - 1),
        (NCH, nz - 1), (NCH, nz - 1), (NCH, NY - 1), (NCH, NY - 1), (NCH,), (NCH,),
        (3, nz), (3, nz), (XCH + 2 * NCH,),
    ]
    anywhere = pl.BlockSpec(memory_space=pl.ANY)
    vmem = pl.BlockSpec(memory_space=pltpu.VMEM)
    merged, lr, wt, bt = pl.pallas_call(
        functools.partial(exchange, nz, 1.0 / replicas),
        out_shape=(
            jax.ShapeDtypeStruct((width, cols), f32),
            jax.ShapeDtypeStruct((width, 2 * RANK), bf16),
            jax.ShapeDtypeStruct((RANK, cols), f32),
            jax.ShapeDtypeStruct((RANK, cols), f32),
        ),
        in_specs=[anywhere, anywhere, anywhere, vmem],
        out_specs=(anywhere, anywhere, vmem, vmem),
        scratch_shapes=[pltpu.VMEM(s, d) for s, d in scratch] + [pltpu.SemaphoreType.DMA(s) for s in sems],
        compiler_params=pltpu.CompilerParams(
            collective_id=0, has_side_effects=True, vmem_limit_bytes=60 * 2**20),
        name="exchange",
    )(inputs, out_grads, error_in[0], basis_in)

    block = width // 8
    share = width // replicas
    index = lax.axis_index("dp").astype(jnp.int32).reshape(1)
    whole = lambda i, s: (0, 0)
    rows = lambda i, s: (i, 0)
    rebuilt, error_out, basis = pl.pallas_call(
        finish,
        out_shape=(
            jax.ShapeDtypeStruct((share, cols), bf16),
            jax.ShapeDtypeStruct((1, width, cols), bf16),
            jax.ShapeDtypeStruct((cols, RANK), f32),
        ),
        grid_spec=pltpu.PrefetchScalarGridSpec(
            num_scalar_prefetch=1,
            grid=(width // block,),
            in_specs=[
                pl.BlockSpec((block, cols), rows),
                pl.BlockSpec((block, 2 * RANK), rows),
                pl.BlockSpec((share, 2 * RANK), lambda i, s: (s[0], 0)),
                pl.BlockSpec((RANK, cols), whole),
                pl.BlockSpec((RANK, cols), whole),
            ],
            out_specs=(
                pl.BlockSpec((share, cols), whole),
                pl.BlockSpec((1, block, cols), lambda i, s: (0, i, 0)),
                pl.BlockSpec((cols, RANK), whole),
            ),
        ),
        name="finish",
    )(index, merged, lr, lr, wt, bt)
    return rebuilt, error_out, basis


def solution(mesh):
    placed = (
        P(("dp", "tensor"), None),
        P("dp", "tensor"),
        P("dp", None, "tensor"),
        P("tensor", None),
    )
    return jax.shard_map(
        shards,
        mesh=mesh,
        in_specs=placed,
        out_specs=(P("dp", "tensor"), P("dp", None, "tensor"), P("tensor", None)),
        check_vma=False,
    )
```

time: 626 us -> 156 us (0.25)
  waiting for transfers between devices: 502 us -> 0 us
  Pallas kernels: 0 us -> 154 us
  matrix products: 63 us -> 0 us
  other arithmetic: 33.2 us -> 0 us
  between operations: 14.1 us -> 0.64 us
  local copies, waits for them, and re-layouts: 6.95 us -> 0 us
    psum x2 -> x0, waiting for transfers between devices: 409 us -> none  [the longest x1 269 us: shards(): low_rank = lax.psum(partial_low, ('dp', 'tensor')) * factor]
    pallas_call x0 -> x2, Pallas kernels: none -> 154 us  [the longest x1 144 us: shards(): pl.pallas_call(functools.partial(exchange, nz, 1.0 / replicas), out_shape...]
    all_gather x1 -> x0, waiting for transfers between devices: 92 us -> none  [shards(): lax.all_gather(inputs, 'tensor', axis=0, tiled=True)]
    dot_general x5 -> x0, matrix products: 57.8 us -> none  [the longest x2 26.8 us: inner_rows(): lax.dot_general(left, right, (((0,), (0,)), ((), ())), precision=highest,...]
    another operation x5 -> x0, other arithmetic: 23 us -> none  [the longest x3 12.4 us: shards(): lower = jnp.linalg.cholesky(gram)]
    broadcast_in_dim x1 -> x0, other arithmetic: 9.24 us -> none  [shards(): error_out = (merged - rebuilt_full).astype(jnp.bfloat16)[None]]
  transfers between devices with their start and end apart: 3 -> 0, of which waited for: 3 -> 0; matrix products, arithmetic and copies ran while one was open for 0% -> 0% of each run, Pallas kernels for 0% -> 0%
where the time goes in v1:
time: 156 us; the launch traced here: 155 us
  Pallas kernels  154 us (99%)
    pallas_call x1, Pallas kernels, shards(): pl.pallas_call(functools.partial(exchange, nz, 1.0 / replicas), out_shape...  144 us
    pallas_call x1, Pallas kernels, shards(): pl.pallas_call(finish, out_shape=(jax.ShapeDtypeStruct((share, cols), bf1...  10.4 us

profile of v1, /device:TPU:2, one launch (start us, length us, event | category | flops | bytes accessed | tf_op | source)
XLA Modules:
  0.0 154.8 jit_solution(426627895629215268)
XLA Ops:
  0.6 143.8 %exchange.1 = (f32[8192,256]{1,0:T(8,128)}, bf16[8192,256]{1,0:T(8,128)(2,1)}, f32[128,256]{1,0:T(8,128)}, f32[128,256]{1,0:T(8,128)}) custom-call(bf16[128,8192]{1,0:T(8,128)(2,1)} %x_hbm.1, bf16[1024,256]{1,0:T(8,128)(2,1)} %g_hbm.1, bf16[8192,256]{1,0:T(8,128)(2,1)} %bitcast.2, f32[256,128]{1,0:T(8,128)} %basis.1), custom_call_target="tpu_custom_call" | custom-call | tf_op jit(solution)/shard_map/exchange/pallas_call | solution.py:401
  144.4 10.4 %finish.1 = (bf16[256,256]{1,0:T(8,128)(2,1)}, bf16[1,8192,256]{2,1,0:T(8,128)(2,1)}, f32[256,128]{1,0:T(8,128)}) custom-call(s32[1]{0:T(128)} %bitcast.index, f32[8192,256]{1,0:T(8,128)} %get-tuple-element.7.merged, bf16[8192,256]{1,0:T(8,128)(2,1)} %get-tuple-element.8.lr.lr_own, bf16[8192,256]{1,0:T(8,128)(2,1)} %get-tuple-element.8.lr.lr_own, ...), custom_call_target="tpu_custom_call" | custom-call | tf_op jit(solution)/shard_map/finish/pallas_call | solution.py:422

commit v2 on v1

v2 whole, which is shorter than its diff:
```python
import functools

import jax
import jax.numpy as jnp
from jax import lax
from jax.experimental import pallas as pl
from jax.experimental.pallas import tpu as pltpu
from jax.sharding import PartitionSpec as P

NX = 4
NY = 4
RANK = 128
NCH = 4
XCH = 16
LAG = 6
OUT = 8
f32, bf16 = jnp.float32, jnp.bfloat16
MESH = pl.DeviceIdType.MESH
OVER_ROWS = (((0,), (0,)), ((), ()))


def split(value):
    high = value.astype(bf16)
    return high, (value - high.astype(f32)).astype(bf16)


def split_columns(value):
    return jnp.concatenate(split(value), axis=1)


def rows_dot(left, right, **kw):
    return lax.dot_general(left, right, OVER_ROWS, preferred_element_type=f32, **kw)


def dot(left, right, **kw):
    return jnp.dot(left, right, preferred_element_type=f32, **kw)


def exchange(
    nz, scale,
    x_hbm, g_hbm, e_hbm, basis,
    merged, lr, wt_ref, bt_ref,
    xg, g, e, p, d2d, yb, zb, xb,
    gb, gbd, gbx, bhl, gbhl,
    u, ub, yt, yb2, yy, yr, gram, aug,
    local, gb_s, gb_r, x_s, x_r, f_s, f_r, sib_s, sib_r,
    d_s, d_r, y_s, y_r, z_s, z_r, xx_s, xx_r,
    za_s, za_r, ya_s, ya_r, da_s, da_r,
    u_s, u_r, q_s, q_r,
):
    width = x_hbm.shape[1]
    tok = x_hbm.shape[0]
    cols = e.shape[1]
    half = width // 2
    hc = half // NCH
    ybl = hc // NY
    zbl = ybl // nz
    cw = width // XCH
    dp = lax.axis_index("dp")
    t = lax.axis_index("tensor")
    z, y = dp // NY, dp % NY
    x, c = t // 2, t % 2
    sib = (dp, x * 2 + (1 - c))

    def at_x(o):
        return lax.rem(x + o + NX, NX)

    def to_x(o):
        return (dp, at_x(o) * 2 + c)

    def at_y(o):
        return lax.rem(y + o, NY)

    def to_y(o):
        return (z * NY + at_y(o), t)

    def at_z(o):
        return lax.rem(z + o, nz)

    def to_z(o):
        return (at_z(o) * NY + y, t)

    sent = []

    def send(src, dst, send_sem, recv_sem, device):
        copy = pltpu.make_async_remote_copy(
            src_ref=src, dst_ref=dst, send_sem=send_sem, recv_sem=recv_sem,
            device_id=device, device_id_type=MESH,
        )
        copy.start()
        sent.append(copy)
        return copy

    load_g = pltpu.make_async_copy(g_hbm, g, local.at[0])
    load_x = pltpu.make_async_copy(x_hbm, xg.at[t], local.at[1])
    load_e = pltpu.make_async_copy(e_hbm, e, local.at[2])
    load_g.start()
    load_x.start()
    load_e.start()

    barrier = pltpu.get_barrier_semaphore()
    partners = [sib] + [to_x(o) for o in range(1, NX)] + [to_y(o) for o in range(1, NY)] + [to_z(o) for o in range(1, nz)]
    for device in partners:
        pl.semaphore_signal(barrier, inc=1, device_id=device, device_id_type=MESH)

    bhl[...] = split_columns(basis[...])
    load_g.wait()
    for block in range(2 * NX):
        product = dot(g[block * tok:(block + 1) * tok, :], bhl[...])
        gb[block % 2, block // 2] = product[:, :RANK] + product[:, RANK:]
    pl.semaphore_wait(barrier, len(partners))
    gb_copy = send(gb.at[1 - c], gbd, gb_s.at[0], gb_r.at[0], sib)
    load_x.wait()

    def chunk_of(shard, j):
        return xg.at[shard, :, pl.ds(j * cw, cw)]

    def own_chunk(j):
        return [
            send(chunk_of(t, j), chunk_of(t, j), x_s.at[j, i], x_r.at[j, i], to_x(o))
            for i, o in enumerate((1, -1))
        ]

    ring = []
    far = [None] * XCH
    to_sib = [[] for _ in range(XCH)]

    def near(j):
        ring[j][0].wait_recv()
        ring[j][1].wait_recv()
        left = chunk_of(at_x(-1) * 2 + c, j)
        right = chunk_of(at_x(1) * 2 + c, j)
        first, last = pl.ds(0, tok // 2), pl.ds(tok // 2, tok // 2)
        far[j] = [
            send(left.at[first], left.at[first], f_s.at[j, 0], f_r.at[j, 0], to_x(1)),
            send(right.at[last], right.at[last], f_s.at[j, 1], f_r.at[j, 1], to_x(-1)),
        ]
        to_sib[j].append(send(left, left, sib_s.at[j, 0], sib_r.at[j, 0], sib))
        to_sib[j].append(send(right, right, sib_s.at[j, 1], sib_r.at[j, 1], sib))

    todo = []
    for j in range(XCH + LAG):
        if j < XCH:
            todo.append(functools.partial(lambda j: ring.append(own_chunk(j)), j))
        if j >= LAG:
            todo.append(functools.partial(near, j - LAG))

    def pump(count=1):
        for _ in range(count):
            if todo:
                todo.pop(0)()

    pump(2)
    gb_copy.wait_recv()
    gb[c] = gb[c] + gbd[...]
    gb_copies = [
        send(gb.at[c, at_x(o)], gbx.at[o - 1], gb_s.at[o], gb_r.at[o], to_x(o)) for o in range(1, NX)
    ]

    own_sib = send(xg.at[t], xg.at[t], sib_s.at[XCH, 0], sib_r.at[XCH, 0], sib)
    pump(2)

    def distant(j):
        for copy in far[j]:
            copy.wait_recv()
        block = chunk_of(at_x(2) * 2 + c, j)
        to_sib[j].append(send(block, block, sib_s.at[j, 2], sib_r.at[j, 2], sib))

    def multiply(j):
        if j == 0:
            own_sib.wait_recv()
        for copy in to_sib[j]:
            copy.wait_recv()
        tile = min(256, cw)

        @pl.loop(0, cw // tile)
        def _(i):
            row = pl.multiple_of(j * cw + i * tile, tile)
            block = xg[:, :, pl.ds(row, tile)].reshape(2 * NX * tok, tile)
            merged[pl.ds(row, tile), :] = rows_dot(block, g[...]) + e[pl.ds(row, tile), :].astype(f32)

    load_e.wait()
    base = min(512, width)

    @pl.loop(0, width // base)
    def _(i):
        row = pl.multiple_of(i * base, base)
        total = dot(e[pl.ds(row, base), :], bhl[...])
        p[pl.ds(row, base), :] = total[:, :RANK] + total[:, RANK:]

    for copy in gb_copies:
        copy.wait_recv()
    gbhl[...] = split_columns(gb[c, x] + gbx[0] + gbx[1] + gbx[2])

    def partial(h, k):
        tile = min(512, hc)

        @pl.loop(0, hc // tile)
        def _(i):
            at = pl.multiple_of(k * hc + i * tile, tile)
            row = pl.multiple_of(h * half + at, tile)
            total = rows_dot(xg[t, :, pl.ds(row, tile)], gbhl[...])
            p[pl.ds(row, tile), :] += total[:, :RANK] + total[:, RANK:]

    def mine(start, size):
        return pl.ds(pl.multiple_of(c * half + start, size), size)

    def theirs(start, size):
        return pl.ds(pl.multiple_of((1 - c) * half + start, size), size)

    y_copies, z_copies, x_copies = {}, {}, {}
    za_copies, ya_copies, da_copies = {}, {}, {}
    d_copies = {}

    def feed_core(k):
        partial(1 - c, k)
        d_copies[k] = send(p.at[theirs(k * hc, hc)], d2d.at[pl.ds(k * hc, hc)], d_s.at[k], d_r.at[k], sib)
        partial(c, k)

    def feed_y(k):
        d_copies[k].wait_recv()
        p[mine(k * hc, hc), :] += d2d[pl.ds(k * hc, hc), :]
        y_copies[k] = [
            send(p.at[mine(k * hc + at_y(o) * ybl, ybl)], yb.at[k, o - 1], y_s.at[k, o - 1], y_r.at[k, o - 1], to_y(o))
            for o in range(1, NY)
        ]

    def own_y(k):
        return mine(k * hc + y * ybl, ybl)

    def own_z(k):
        return mine(k * hc + y * ybl + z * zbl, zbl)

    def stage_y(k):
        for copy in y_copies[k]:
            copy.wait_recv()
        total = p[own_y(k), :]
        for i in range(NY - 1):
            total = total + yb[k, i]
        p[own_y(k), :] = total
        z_copies[k] = [
            send(p.at[mine(k * hc + y * ybl + at_z(o) * zbl, zbl)], zb.at[k, o - 1],
                 z_s.at[k, o - 1], z_r.at[k, o - 1], to_z(o))
            for o in range(1, nz)
        ]

    def stage_z(k):
        for copy in z_copies[k]:
            copy.wait_recv()
        total = p[own_z(k), :]
        for i in range(nz - 1):
            total = total + zb[k, i]
        xb[k, x] = total
        x_copies[k] = [
            send(xb.at[k, x], xb.at[k, x], xx_s.at[k, o - 1], xx_r.at[k, o - 1], to_x(o)) for o in range(1, NX)
        ]

    def stage_x(k):
        for copy in x_copies[k]:
            copy.wait_recv()
        total = xb[k, 0]
        for i in range(1, NX):
            total = total + xb[k, i]
        lr[own_z(k), :] = split_columns(total * scale)
        block = lr.at[own_z(k)]
        za_copies[k] = [
            send(block, block, za_s.at[k, o - 1], za_r.at[k, o - 1], to_z(o)) for o in range(1, nz)
        ]

    def gather_z(k):
        for copy in za_copies[k]:
            copy.wait_recv()
        block = lr.at[own_y(k)]
        ya_copies[k] = [
            send(block, block, ya_s.at[k, o - 1], ya_r.at[k, o - 1], to_y(o)) for o in range(1, NY)
        ]

    def gather_y(k):
        for copy in ya_copies[k]:
            copy.wait_recv()
        block = lr.at[mine(k * hc, hc)]
        da_copies[k] = send(block, block, da_s.at[k], da_r.at[k], sib)

    def gather_core(k):
        da_copies[k].wait_recv()
        tile = min(512, hc)
        for h in range(2):
            @pl.loop(0, hc // tile)
            def _(i):
                row = pl.multiple_of(h * half + k * hc + i * tile, tile)
                pair = lr[pl.ds(row, tile), :]
                both = rows_dot(pair, e[pl.ds(row, tile), :])
                yt[...] += both[:RANK] + both[RANK:]
                u[...] += dot(xg[t, :, pl.ds(row, tile)], pair)
                square = rows_dot(pair, pair)
                gram[...] += (square[:RANK, :RANK] + square[RANK:, RANK:]) + (square[:RANK, RANK:] + square[RANK:, :RANK])

    yt[...] = jnp.zeros_like(yt)
    u[...] = jnp.zeros_like(u)
    gram[...] = jnp.zeros_like(gram)
    stages = (feed_core, feed_y, stage_y, stage_z, stage_x, gather_z, gather_y, gather_core)
    lags = (0, 1, 3, 4, 5, 6, 7, 8)
    for s in range(NCH + lags[-1]):
        for stage, lag in zip(stages, lags):
            if 0 <= s - lag < NCH:
                stage(s - lag)
                pump()
    pump(len(todo))

    lane = lax.broadcasted_iota(jnp.int32, (RANK, 2 * RANK), 1)
    sub = lax.broadcasted_iota(jnp.int32, (RANK, 2 * RANK), 0)
    aug[:, :RANK] = gram[...]
    aug[:, RANK:] = jnp.where(
        lax.broadcasted_iota(jnp.int32, (RANK, RANK), 0) == lax.broadcasted_iota(jnp.int32, (RANK, RANK), 1), 1.0, 0.0)

    def eliminate(first, last):
        @pl.loop(first, last)
        def _(j):
            row = aug[pl.ds(j, 1), :]
            pivot = jnp.sum(jnp.where(lane[:1] == j, row, 0.0), axis=1, keepdims=True)
            column = jnp.sum(jnp.where(lane == j, aug[...], 0.0), axis=1, keepdims=True)
            factor = jnp.where(sub[:, :1] > j, column / pivot, 0.0)
            aug[...] = aug[...] - factor * row

    ub[c, x] = u[:, :RANK] + u[:, RANK:]
    copies = [send(ub.at[c, x], ub.at[c, x], u_s.at[o], u_r.at[o], to_x(o)) for o in range(1, NX)]
    cuts = (0, RANK // 4, RANK // 2, 3 * RANK // 4, RANK)
    eliminate(cuts[0], cuts[1])
    for j in range(12):
        distant(j)
    for copy in copies:
        copy.wait_recv()
    u_copy = send(ub.at[c], ub.at[c], u_s.at[0], u_r.at[0], sib)
    for j in range(0, 3):
        multiply(j)
    u_copy.wait_recv()
    for core in range(2):
        for chip in range(NX):
            token = (chip * 2 + core) * tok
            both = rows_dot(split_columns(ub[core, chip]), g[token:token + tok, :])
            yt[...] += both[:RANK] + both[RANK:]

    part = RANK // NY
    own = pl.ds(pl.multiple_of(y * part, part), part)
    copies = [
        send(yt.at[pl.ds(pl.multiple_of(at_y(o) * part, part), part)], yb2.at[o - 1], q_s.at[0, o], q_r.at[0, o], to_y(o))
        for o in range(1, NY)
    ]
    for j in range(3, 6):
        multiply(j)
    eliminate(cuts[1], cuts[2])
    for copy in copies:
        copy.wait_recv()
    total = yt[own, :]
    for i in range(NY - 1):
        total = total + yb2[i]
    yy[z] = total
    copies = [send(yy.at[z], yy.at[z], q_s.at[1, o], q_r.at[1, o], to_z(o)) for o in range(1, nz)]
    eliminate(cuts[2], cuts[3])
    for j in range(6, 10):
        multiply(j)
    for copy in copies:
        copy.wait_recv()
    total = yy[0]
    for i in range(1, nz):
        total = total + yy[i]
    yr[own, :] = total * scale
    copies = [send(yr.at[own], yr.at[own], q_s.at[2, o], q_r.at[2, o], to_y(o)) for o in range(1, NY)]
    eliminate(cuts[3], cuts[4])
    pivots = jnp.sum(jnp.where(lane == sub, aug[...], 0.0), axis=1, keepdims=True)
    inverse = aug[:, RANK:] / jnp.sqrt(pivots)
    for copy in copies:
        copy.wait_recv()
    bt = dot(inverse, yr[...], precision=lax.Precision.HIGHEST)
    bt_ref[...] = bt
    wt_ref[...] = rows_dot(inverse, bt, precision=lax.Precision.HIGHEST)
    for j in range(12, XCH):
        distant(j)
    for j in range(10, XCH):
        multiply(j)
    for copy in sent:
        copy.wait_send()


def finish(merged, lr, wt, bt, rebuilt_ref, error_hbm, basis_ref, out, sems):
    dp = lax.axis_index("dp")
    width = merged.shape[0]
    share = rebuilt_ref.shape[0]
    high, low = split(wt[...])
    twice = jnp.concatenate([high, high], axis=0)

    def rebuild(pair):
        return dot(pair, twice) + dot(pair[:, :RANK], low)

    block = width // OUT
    tile = min(256, block)
    copies = []
    for j in range(OUT):
        @pl.loop(0, block // tile)
        def _(i):
            row = pl.multiple_of(j * block + i * tile, tile)
            rows = pl.ds(row, tile)
            out[rows, :] = (merged[rows, :] - rebuild(lr[rows, :])).astype(bf16)

        rows = pl.ds(j * block, block)
        copy = pltpu.make_async_copy(out.at[rows], error_hbm.at[0, rows], sems.at[j])
        copy.start()
        copies.append(copy)
    rebuilt_ref[...] = rebuild(lr[pl.ds(pl.multiple_of(dp * share, share), share), :]).astype(bf16)
    basis_ref[...] = bt[...].T
    for copy in copies:
        copy.wait()


def shards(inputs, out_grads, error_in, basis_in):
    replicas = lax.axis_size("dp")
    nz = replicas // NY
    tok, width = inputs.shape
    tokens, cols = out_grads.shape
    half = width // 2
    hc = half // NCH
    ybl = hc // NY
    zbl = ybl // nz
    scratch = [
        ((2 * NX, tok, width), bf16),
        ((tokens, cols), bf16),
        ((width, cols), bf16),
        ((width, RANK), f32),
        ((half, RANK), f32),
        ((NCH, NY - 1, ybl, RANK), f32),
        ((NCH, nz - 1, zbl, RANK), f32),
        ((NCH, NX, zbl, RANK), f32),
        ((2, NX, tok, RANK), f32),
        ((NX, tok, RANK), f32),
        ((NX - 1, tok, RANK), f32),
        ((cols, 2 * RANK), bf16),
        ((tok, 2 * RANK), bf16),
        ((tok, 2 * RANK), f32),
        ((2, NX, tok, RANK), f32),
        ((RANK, cols), f32),
        ((NY - 1, RANK // NY, cols), f32),
        ((nz, RANK // NY, cols), f32),
        ((RANK, cols), f32),
        ((RANK, RANK), f32),
        ((RANK, 2 * RANK), f32),
    ]
    sems = [
        (3,), (NX,), (NX,), (XCH, 2), (XCH, 2), (XCH, 2), (XCH, 2), (XCH + 1, 3), (XCH + 1, 3),
        (NCH,), (NCH,), (NCH, NY - 1), (NCH, NY - 1), (NCH, nz - 1), (NCH, nz - 1), (NCH, NX - 1), (NCH, NX - 1),
        (NCH, nz - 1), (NCH, nz - 1), (NCH, NY - 1), (NCH, NY - 1), (NCH,), (NCH,),
        (NX,), (NX,), (3, nz), (3, nz),
    ]
    anywhere = pl.BlockSpec(memory_space=pl.ANY)
    vmem = pl.BlockSpec(memory_space=pltpu.VMEM)
    merged, lr, wt, bt = pl.pallas_call(
        functools.partial(exchange, nz, 1.0 / replicas),
        out_shape=(
            pltpu.VMEM((width, cols), f32),
            pltpu.VMEM((width, 2 * RANK), bf16),
            pltpu.VMEM((RANK, cols), f32),
            pltpu.VMEM((RANK, cols), f32),
        ),
        in_specs=[anywhere, anywhere, anywhere, vmem],
        out_specs=(vmem,) * 4,
        scratch_shapes=[pltpu.VMEM(s, d) for s, d in scratch] + [pltpu.SemaphoreType.DMA(s) for s in sems],
        compiler_params=pltpu.CompilerParams(
            collective_id=0, has_side_effects=True, vmem_limit_bytes=42 * 2**20),
        name="exchange",
    )(inputs, out_grads, error_in[0], basis_in)

    share = width // replicas
    rebuilt, error_out, basis = pl.pallas_call(
        finish,
        out_shape=(
            jax.ShapeDtypeStruct((share, cols), bf16),
            jax.ShapeDtypeStruct((1, width, cols), bf16),
            jax.ShapeDtypeStruct((cols, RANK), f32),
        ),
        in_specs=[vmem] * 4,
        out_specs=(vmem, anywhere, vmem),
        scratch_shapes=[pltpu.VMEM((width, cols), bf16), pltpu.SemaphoreType.DMA((OUT,))],
        compiler_params=pltpu.CompilerParams(vmem_limit_bytes=12 * 2**20),
        name="finish",
    )(merged, lr, wt, bt)
    return rebuilt, error_out, basis


def solution(mesh):
    placed = (
        P(("dp", "tensor"), None),
        P("dp", "tensor"),
        P("dp", None, "tensor"),
        P("tensor", None),
    )
    return jax.shard_map(
        shards,
        mesh=mesh,
        in_specs=placed,
        out_specs=(P("dp", "tensor"), P("dp", None, "tensor"), P("tensor", None)),
        check_vma=False,
    )
```

time: 156 us -> 131 us (0.84)
  Pallas kernels: 154 us -> 128 us
    pallas_call x1, Pallas kernels: 144 us -> 119 us  [shards(): pl.pallas_call(functools.partial(exchange, nz, 1.0 / replicas), out_shape...]
    pallas_call x1, Pallas kernels: 10.4 us -> 8.56 us  [shards(): pl.pallas_call(finish, out_shape=(jax.ShapeDtypeStruct((share, cols), bf1...]
where the time goes in v2:
time: 131 us; the launch traced here: 129 us
  Pallas kernels  128 us (98%)
    pallas_call x1, Pallas kernels, shards(): pl.pallas_call(functools.partial(exchange, nz, 1.0 / replicas), out_shape...  119 us
    pallas_call x1, Pallas kernels, shards(): pl.pallas_call(finish, out_shape=(jax.ShapeDtypeStruct((share, cols), bf1...  8.56 us

profile of v2, /device:TPU:2, one launch (start us, length us, event | category | flops | bytes accessed | tf_op | source)
XLA Modules:
  0.0 128.7 jit_solution(12033309772502052760)
XLA Ops:
  0.6 119.5 %exchange.1 = (f32[8192,256]{1,0:T(8,128)S(1)}, bf16[8192,256]{1,0:T(8,128)(2,1)S(1)}, f32[128,256]{1,0:T(8,128)S(1)}, f32[128,256]{1,0:T(8,128)S(1)}) custom-call(bf16[128,8192]{1,0:T(8,128)(2,1)} %x_hbm.1, bf16[1024,256]{1,0:T(8,128)(2,1)} %g_hbm.1, bf16[8192,256]{1,0:T(8,128)(2,1)} %bitcast.1, f32[256,128]{1,0:T(8,128)} %basis.1), custom_call_target="tpu_custom_call" | custom-call | tf_op jit(solution)/shard_map/exchange/pallas_call | solution.py:455
  120.1 8.6 %finish.1 = (bf16[256,256]{1,0:T(8,128)(2,1)}, bf16[1,8192,256]{2,1,0:T(8,128)(2,1)}, f32[256,128]{1,0:T(8,128)}) custom-call(f32[8192,256]{1,0:T(8,128)S(1)} %get-tuple-element.7.merged, bf16[8192,256]{1,0:T(8,128)(2,1)S(1)} %get-tuple-element.8.lr, f32[128,256]{1,0:T(8,128)S(1)} %get-tuple-element.9.wt, f32[128,256]{1,0:T(8,128)S(1)} %get-tuple-element.10.bt), custom_call_target="tpu_custom_call" | custom-call | tf_op jit(solution)/shard_map/finish/pallas_call | solution.py:472

commit v3 on v2

--- a/solution.py
+++ b/solution.py
@@ -12,11 +12,22 @@
 RANK = 128
 NCH = 4
 XCH = 16
+Z_FIRST = ()
 LAG = 6
+FAR, FULL = 4, 6
+PUMP0, PUMP1 = 1, 1
 OUT = 8
 f32, bf16 = jnp.float32, jnp.bfloat16
 MESH = pl.DeviceIdType.MESH
 OVER_ROWS = (((0,), (0,)), ((), ()))
+
+
+def timetable():
+    lags = (0, 1, 3, 4, 5, 6, 7, 8)
+    return [
+        (stage, step - lag)
+        for step in range(NCH + lags[-1]) for stage, lag in enumerate(lags) if 0 <= step - lag < NCH
+    ]
 
 
 def split(value):
@@ -116,10 +127,10 @@
         return xg.at[shard, :, pl.ds(j * cw, cw)]
 
     def own_chunk(j):
-        return [
+        ring.append([
             send(chunk_of(t, j), chunk_of(t, j), x_s.at[j, i], x_r.at[j, i], to_x(o))
             for i, o in enumerate((1, -1))
-        ]
+        ])
 
     ring = []
     far = [None] * XCH
@@ -138,19 +149,45 @@
         to_sib[j].append(send(left, left, sib_s.at[j, 0], sib_r.at[j, 0], sib))
         to_sib[j].append(send(right, right, sib_s.at[j, 1], sib_r.at[j, 1], sib))
 
+    def distant(j):
+        for copy in far[j]:
+            copy.wait_recv()
+        block = chunk_of(at_x(2) * 2 + c, j)
+        to_sib[j].append(send(block, block, sib_s.at[j, 2], sib_r.at[j, 2], sib))
+
+    def multiply(j):
+        if j == 0:
+            own_sib.wait_recv()
+        for copy in to_sib[j]:
+            copy.wait_recv()
+        tile = min(256, cw)
+
+        @pl.loop(0, cw // tile)
+        def _(i):
+            row = pl.multiple_of(j * cw + i * tile, tile)
+            block = xg[:, :, pl.ds(row, tile)].reshape(2 * NX * tok, tile)
+            merged[pl.ds(row, tile), :] = rows_dot(block, g[...]) + e[pl.ds(row, tile), :].astype(f32)
+
+    def forward(j):
+        if j >= FAR:
+            distant(j - FAR)
+        near(j)
+        if j >= FULL:
+            multiply(j - FULL)
+
     todo = []
     for j in range(XCH + LAG):
         if j < XCH:
-            todo.append(functools.partial(lambda j: ring.append(own_chunk(j)), j))
+            todo.append(functools.partial(own_chunk, j))
         if j >= LAG:
-            todo.append(functools.partial(near, j - LAG))
+            todo.append(functools.partial(forward, j - LAG))
 
     def pump(count=1):
         for _ in range(count):
             if todo:
                 todo.pop(0)()
 
-    pump(2)
+    pump(PUMP0)
     gb_copy.wait_recv()
     gb[c] = gb[c] + gbd[...]
     gb_copies = [
@@ -158,26 +195,7 @@
     ]
 
     own_sib = send(xg.at[t], xg.at[t], sib_s.at[XCH, 0], sib_r.at[XCH, 0], sib)
-    pump(2)
-
-    def distant(j):
-        for copy in far[j]:
-            copy.wait_recv()
-        block = chunk_of(at_x(2) * 2 + c, j)
-        to_sib[j].append(send(block, block, sib_s.at[j, 2], sib_r.at[j, 2], sib))
-
-    def multiply(j):
-        if j == 0:
-            own_sib.wait_recv()
-        for copy in to_sib[j]:
-            copy.wait_recv()
-        tile = min(256, cw)
-
-        @pl.loop(0, cw // tile)
-        def _(i):
-            row = pl.multiple_of(j * cw + i * tile, tile)
-            block = xg[:, :, pl.ds(row, tile)].reshape(2 * NX * tok, tile)
-            merged[pl.ds(row, tile), :] = rows_dot(block, g[...]) + e[pl.ds(row, tile), :].astype(f32)
+    pump(PUMP1)
 
     load_e.wait()
     base = min(512, width)
@@ -217,39 +235,59 @@
         d_copies[k] = send(p.at[theirs(k * hc, hc)], d2d.at[pl.ds(k * hc, hc)], d_s.at[k], d_r.at[k], sib)
         partial(c, k)
 
-    def feed_y(k):
+    over_y = (NY, to_y, at_y, y)
+    over_z = (nz, to_z, at_z, z)
+
+    def axes(k):
+        return (over_z, over_y) if k in Z_FIRST else (over_y, over_z)
+
+    def first_block(k, index):
+        size = hc // axes(k)[0][0]
+        return mine(k * hc + index * size, size)
+
+    def second_block(k, index):
+        (n1, _, _, own1), (n2, _, _, _) = axes(k)
+        size = hc // n1 // n2
+        return mine(k * hc + own1 * (hc // n1) + index * size, size)
+
+    def own_first(k):
+        return first_block(k, axes(k)[0][3])
+
+    def own_second(k):
+        return second_block(k, axes(k)[1][3])
+
+    def feed_first(k):
         d_copies[k].wait_recv()
         p[mine(k * hc, hc), :] += d2d[pl.ds(k * hc, hc), :]
+        n, to, at, _ = axes(k)[0]
+        size = hc // n
         y_copies[k] = [
-            send(p.at[mine(k * hc + at_y(o) * ybl, ybl)], yb.at[k, o - 1], y_s.at[k, o - 1], y_r.at[k, o - 1], to_y(o))
-            for o in range(1, NY)
+            send(p.at[first_block(k, at(o))], yb.at[k, pl.ds((o - 1) * size, size)], y_s.at[k, o - 1], y_r.at[k, o - 1], to(o))
+            for o in range(1, n)
         ]
 
-    def own_y(k):
-        return mine(k * hc + y * ybl, ybl)
-
-    def own_z(k):
-        return mine(k * hc + y * ybl + z * zbl, zbl)
-
-    def stage_y(k):
+    def stage_first(k):
         for copy in y_copies[k]:
             copy.wait_recv()
-        total = p[own_y(k), :]
-        for i in range(NY - 1):
-            total = total + yb[k, i]
-        p[own_y(k), :] = total
+        n, to, at, _ = axes(k)[0]
+        size = hc // n
+        total = p[own_first(k), :]
+        for i in range(n - 1):
+            total = total + yb[k, i * size:(i + 1) * size, :]
+        p[own_first(k), :] = total
+        n, to, at, _ = axes(k)[1]
+        size = zbl
         z_copies[k] = [
-            send(p.at[mine(k * hc + y * ybl + at_z(o) * zbl, zbl)], zb.at[k, o - 1],
-                 z_s.at[k, o - 1], z_r.at[k, o - 1], to_z(o))
-            for o in range(1, nz)
+            send(p.at[second_block(k, at(o))], zb.at[k, pl.ds((o - 1) * size, size)], z_s.at[k, o - 1], z_r.at[k, o - 1], to(o))
+            for o in range(1, n)
         ]
 
-    def stage_z(k):
+    def stage_second(k):
         for copy in z_copies[k]:
             copy.wait_recv()
-        total = p[own_z(k), :]
-        for i in range(nz - 1):
-            total = total + zb[k, i]
+        total = p[own_second(k), :]
+        for i in range(axes(k)[1][0] - 1):
+            total = total + zb[k, i * zbl:(i + 1) * zbl, :]
         xb[k, x] = total
         x_copies[k] = [
             send(xb.at[k, x], xb.at[k, x], xx_s.at[k, o - 1], xx_r.at[k, o - 1], to_x(o)) for o in range(1, NX)
@@ -261,21 +299,23 @@
         total = xb[k, 0]
         for i in range(1, NX):
             total = total + xb[k, i]
-        lr[own_z(k), :] = split_columns(total * scale)
-        block = lr.at[own_z(k)]
+        lr[own_second(k), :] = split_columns(total * scale)
+        block = lr.at[own_second(k)]
+        n, to, _, _ = axes(k)[1]
         za_copies[k] = [
-            send(block, block, za_s.at[k, o - 1], za_r.at[k, o - 1], to_z(o)) for o in range(1, nz)
+            send(block, block, za_s.at[k, o - 1], za_r.at[k, o - 1], to(o)) for o in range(1, n)
         ]
 
-    def gather_z(k):
+    def gather_second(k):
         for copy in za_copies[k]:
             copy.wait_recv()
-        block = lr.at[own_y(k)]
+        block = lr.at[own_first(k)]
+        n, to, _, _ = axes(k)[0]
         ya_copies[k] = [
-            send(block, block, ya_s.at[k, o - 1], ya_r.at[k, o - 1], to_y(o)) for o in range(1, NY)
+            send(block, block, ya_s.at[k, o - 1], ya_r.at[k, o - 1], to(o)) for o in range(1, n)
         ]
 
-    def gather_y(k):
+    def gather_first(k):
         for copy in ya_copies[k]:
             copy.wait_recv()
         block = lr.at[mine(k * hc, hc)]
@@ -298,13 +338,10 @@
     yt[...] = jnp.zeros_like(yt)
     u[...] = jnp.zeros_like(u)
     gram[...] = jnp.zeros_like(gram)
-    stages = (feed_core, feed_y, stage_y, stage_z, stage_x, gather_z, gather_y, gather_core)
-    lags = (0, 1, 3, 4, 5, 6, 7, 8)
-    for s in range(NCH + lags[-1]):
-        for stage, lag in zip(stages, lags):
-            if 0 <= s - lag < NCH:
-                stage(s - lag)
-                pump()
+    stages = (feed_core, feed_first, stage_first, stage_second, stage_x, gather_second, gather_first, gather_core)
+    for stage, k in timetable():
+        stages[stage](k)
+        pump()
     pump(len(todo))
 
     lane = lax.broadcasted_iota(jnp.int32, (RANK, 2 * RANK), 1)
@@ -326,13 +363,14 @@
     copies = [send(ub.at[c, x], ub.at[c, x], u_s.at[o], u_r.at[o], to_x(o)) for o in range(1, NX)]
     cuts = (0, RANK // 4, RANK // 2, 3 * RANK // 4, RANK)
     eliminate(cuts[0], cuts[1])
-    for j in range(12):
+    rest = list(range(XCH - FULL, XCH))
+    for j in range(XCH - FAR, XCH - 2):
         distant(j)
+    multiply(rest.pop(0))
     for copy in copies:
         copy.wait_recv()
     u_copy = send(ub.at[c], ub.at[c], u_s.at[0], u_r.at[0], sib)
-    for j in range(0, 3):
-        multiply(j)
+    multiply(rest.pop(0))
     u_copy.wait_recv()
     for core in range(2):
         for chip in range(NX):
@@ -346,9 +384,9 @@
         send(yt.at[pl.ds(pl.multiple_of(at_y(o) * part, part), part)], yb2.at[o - 1], q_s.at[0, o], q_r.at[0, o], to_y(o))
         for o in range(1, NY)
     ]
-    for j in range(3, 6):
-        multiply(j)
     eliminate(cuts[1], cuts[2])
+    for j in range(XCH - 2, XCH):
+        distant(j)
     for copy in copies:
         copy.wait_recv()
     total = yt[own, :]
@@ -357,8 +395,8 @@
     yy[z] = total
     copies = [send(yy.at[z], yy.at[z], q_s.at[1, o], q_r.at[1, o], to_z(o)) for o in range(1, nz)]
     eliminate(cuts[2], cuts[3])
-    for j in range(6, 10):
-        multiply(j)
+    multiply(rest.pop(0))
+    multiply(rest.pop(0))
     for copy in copies:
         copy.wait_recv()
     total = yy[0]
@@ -374,9 +412,7 @@
     bt = dot(inverse, yr[...], precision=lax.Precision.HIGHEST)
     bt_ref[...] = bt
     wt_ref[...] = rows_dot(inverse, bt, precision=lax.Precision.HIGHEST)
-    for j in range(12, XCH):
-        distant(j)
-    for j in range(10, XCH):
+    for j in rest:
         multiply(j)
     for copy in sent:
         copy.wait_send()
@@ -393,7 +429,7 @@
         return dot(pair, twice) + dot(pair[:, :RANK], low)
 
     block = width // OUT
-    tile = min(256, block)
+    tile = min(512, block)
     copies = []
     for j in range(OUT):
         @pl.loop(0, block // tile)
@@ -427,8 +463,8 @@
         ((width, cols), bf16),
         ((width, RANK), f32),
         ((half, RANK), f32),
-        ((NCH, NY - 1, ybl, RANK), f32),
-        ((NCH, nz - 1, zbl, RANK), f32),
+        ((NCH, hc, RANK), f32),
+        ((NCH, hc // NY, RANK), f32),
         ((NCH, NX, zbl, RANK), f32),
         ((2, NX, tok, RANK), f32),
         ((NX, tok, RANK), f32),
@@ -446,8 +482,8 @@
     ]
     sems = [
         (3,), (NX,), (NX,), (XCH, 2), (XCH, 2), (XCH, 2), (XCH, 2), (XCH + 1, 3), (XCH + 1, 3),
-        (NCH,), (NCH,), (NCH, NY - 1), (NCH, NY - 1), (NCH, nz - 1), (NCH, nz - 1), (NCH, NX - 1), (NCH, NX - 1),
-        (NCH, nz - 1), (NCH, nz - 1), (NCH, NY - 1), (NCH, NY - 1), (NCH,), (NCH,),
+        (NCH,), (NCH,), (NCH, nz - 1), (NCH, nz - 1), (NCH, nz - 1), (NCH, nz - 1), (NCH, NX - 1), (NCH, NX - 1),
+        (NCH, nz - 1), (NCH, nz - 1), (NCH, nz - 1), (NCH, nz - 1), (NCH,), (NCH,),
         (NX,), (NX,), (3, nz), (3, nz),
     ]
     anywhere = pl.BlockSpec(memory_space=pl.ANY)

time: 131 us -> 123 us (0.939)
  Pallas kernels: 128 us -> 121 us
    pallas_call x1, Pallas kernels: 119 us -> 115 us  [shards(): pl.pallas_call(functools.partial(exchange, nz, 1.0 / replicas), out_shape...]
    pallas_call x1, Pallas kernels: 8.56 us -> 6.17 us  [shards(): pl.pallas_call(finish, out_shape=(jax.ShapeDtypeStruct((share, cols), bf1...]
where the time goes in v3:
time: 123 us; the launch traced here: 121 us
  Pallas kernels  121 us (98%)
    pallas_call x1, Pallas kernels, shards(): pl.pallas_call(functools.partial(exchange, nz, 1.0 / replicas), out_shape...  115 us
    pallas_call x1, Pallas kernels, shards(): pl.pallas_call(finish, out_shape=(jax.ShapeDtypeStruct((share, cols), bf1...  6.17 us

profile of v3, /device:TPU:2, one launch (start us, length us, event | category | flops | bytes accessed | tf_op | source)
XLA Modules:
  0.0 121.3 jit_solution(7102475674211506068)
XLA Ops:
  0.6 114.5 %exchange.1 = (f32[8192,256]{1,0:T(8,128)S(1)}, bf16[8192,256]{1,0:T(8,128)(2,1)S(1)}, f32[128,256]{1,0:T(8,128)S(1)}, f32[128,256]{1,0:T(8,128)S(1)}) custom-call(bf16[128,8192]{1,0:T(8,128)(2,1)} %x_hbm.1, bf16[1024,256]{1,0:T(8,128)(2,1)} %g_hbm.1, bf16[8192,256]{1,0:T(8,128)(2,1)} %bitcast.1, f32[256,128]{1,0:T(8,128)} %basis.1), custom_call_target="tpu_custom_call" | custom-call | tf_op jit(solution)/shard_map/exchange/pallas_call | solution.py:491
  115.2 6.2 %finish.1 = (bf16[256,256]{1,0:T(8,128)(2,1)}, bf16[1,8192,256]{2,1,0:T(8,128)(2,1)}, f32[256,128]{1,0:T(8,128)}) custom-call(f32[8192,256]{1,0:T(8,128)S(1)} %get-tuple-element.7.merged, bf16[8192,256]{1,0:T(8,128)(2,1)S(1)} %get-tuple-element.8.lr, f32[128,256]{1,0:T(8,128)S(1)} %get-tuple-element.9.wt, f32[128,256]{1,0:T(8,128)S(1)} %get-tuple-element.10.bt), custom_call_target="tpu_custom_call" | custom-call | tf_op jit(solution)/shard_map/finish/pallas_call | solution.py:508

commit v4 on v3

--- a/solution.py
+++ b/solution.py
@@ -16,18 +16,11 @@
 LAG = 6
 FAR, FULL = 4, 6
 PUMP0, PUMP1 = 1, 1
+PUMPS = (2, 2, 2, 3, 3, 3, 3, 3, 3, 3, 3, 3)
 OUT = 8
 f32, bf16 = jnp.float32, jnp.bfloat16
 MESH = pl.DeviceIdType.MESH
 OVER_ROWS = (((0,), (0,)), ((), ()))
-
-
-def timetable():
-    lags = (0, 1, 3, 4, 5, 6, 7, 8)
-    return [
-        (stage, step - lag)
-        for step in range(NCH + lags[-1]) for stage, lag in enumerate(lags) if 0 <= step - lag < NCH
-    ]
 
 
 def split(value):
@@ -160,7 +153,7 @@
             own_sib.wait_recv()
         for copy in to_sib[j]:
             copy.wait_recv()
-        tile = min(256, cw)
+        tile = min(512, cw)
 
         @pl.loop(0, cw // tile)
         def _(i):
@@ -339,9 +332,12 @@
     u[...] = jnp.zeros_like(u)
     gram[...] = jnp.zeros_like(gram)
     stages = (feed_core, feed_first, stage_first, stage_second, stage_x, gather_second, gather_first, gather_core)
-    for stage, k in timetable():
-        stages[stage](k)
-        pump()
+    lags = (0, 1, 3, 4, 5, 6, 7, 8)
+    for s in range(NCH + lags[-1]):
+        for stage, lag in tuple(zip(stages, lags))[::-1]:
+            if 0 <= s - lag < NCH:
+                stage(s - lag)
+        pump(PUMPS[s])
     pump(len(todo))
 
     lane = lax.broadcasted_iota(jnp.int32, (RANK, 2 * RANK), 1)
@@ -354,11 +350,18 @@
         @pl.loop(first, last)
         def _(j):
             row = aug[pl.ds(j, 1), :]
-            pivot = jnp.sum(jnp.where(lane[:1] == j, row, 0.0), axis=1, keepdims=True)
-            column = jnp.sum(jnp.where(lane == j, aug[...], 0.0), axis=1, keepdims=True)
+            pivot = jnp.sum(jnp.where(lane[:1, :RANK] == j, row[:, :RANK], 0.0), axis=1, keepdims=True)
+            column = jnp.sum(jnp.where(lane[:, :RANK] == j, aug[:, :RANK], 0.0), axis=1, keepdims=True)
             factor = jnp.where(sub[:, :1] > j, column / pivot, 0.0)
             aug[...] = aug[...] - factor * row
 
+    early = list(sent)
+
+    def finished(shares):
+        for _ in range(-(-len(early) // shares)):
+            early.pop(0).wait_send()
+
+    last = len(sent)
     ub[c, x] = u[:, :RANK] + u[:, RANK:]
     copies = [send(ub.at[c, x], ub.at[c, x], u_s.at[o], u_r.at[o], to_x(o)) for o in range(1, NX)]
     cuts = (0, RANK // 4, RANK // 2, 3 * RANK // 4, RANK)
@@ -370,6 +373,7 @@
     for copy in copies:
         copy.wait_recv()
     u_copy = send(ub.at[c], ub.at[c], u_s.at[0], u_r.at[0], sib)
+    finished(3)
     multiply(rest.pop(0))
     u_copy.wait_recv()
     for core in range(2):
@@ -384,6 +388,7 @@
         send(yt.at[pl.ds(pl.multiple_of(at_y(o) * part, part), part)], yb2.at[o - 1], q_s.at[0, o], q_r.at[0, o], to_y(o))
         for o in range(1, NY)
     ]
+    finished(2)
     eliminate(cuts[1], cuts[2])
     for j in range(XCH - 2, XCH):
         distant(j)
@@ -394,6 +399,7 @@
         total = total + yb2[i]
     yy[z] = total
     copies = [send(yy.at[z], yy.at[z], q_s.at[1, o], q_r.at[1, o], to_z(o)) for o in range(1, nz)]
+    finished(1)
     eliminate(cuts[2], cuts[3])
     multiply(rest.pop(0))
     multiply(rest.pop(0))
@@ -414,7 +420,7 @@
     wt_ref[...] = rows_dot(inverse, bt, precision=lax.Precision.HIGHEST)
     for j in rest:
         multiply(j)
-    for copy in sent:
+    for copy in early + sent[last:]:
         copy.wait_send()
 
 

time: 123 us -> 121 us (0.984)
  Pallas kernels: 121 us -> 118 us
    pallas_call x1, Pallas kernels: 115 us -> 112 us  [shards(): pl.pallas_call(functools.partial(exchange, nz, 1.0 / replicas), out_shape...]
where the time goes in v4:
time: 121 us; the launch traced here: 119 us
  Pallas kernels  118 us (98%)
    pallas_call x1, Pallas kernels, shards(): pl.pallas_call(functools.partial(exchange, nz, 1.0 / replicas), out_shape...  112 us
    pallas_call x1, Pallas kernels, shards(): pl.pallas_call(finish, out_shape=(jax.ShapeDtypeStruct((share, cols), bf1...  6.17 us

profile of v4, /device:TPU:2, one launch (start us, length us, event | category | flops | bytes accessed | tf_op | source)
XLA Modules:
  0.0 119.0 jit_solution(2629264572241657159)
XLA Ops:
  0.6 112.0 %exchange.1 = (f32[8192,256]{1,0:T(8,128)S(1)}, bf16[8192,256]{1,0:T(8,128)(2,1)S(1)}, f32[128,256]{1,0:T(8,128)S(1)}, f32[128,256]{1,0:T(8,128)S(1)}) custom-call(bf16[128,8192]{1,0:T(8,128)(2,1)} %x_hbm.1, bf16[1024,256]{1,0:T(8,128)(2,1)} %g_hbm.1, bf16[8192,256]{1,0:T(8,128)(2,1)} %bitcast.1, f32[256,128]{1,0:T(8,128)} %basis.1), custom_call_target="tpu_custom_call" | custom-call | tf_op jit(solution)/shard_map/exchange/pallas_call | solution.py:497
  112.7 6.2 %finish.1 = (bf16[256,256]{1,0:T(8,128)(2,1)}, bf16[1,8192,256]{2,1,0:T(8,128)(2,1)}, f32[256,128]{1,0:T(8,128)}) custom-call(f32[8192,256]{1,0:T(8,128)S(1)} %get-tuple-element.7.merged, bf16[8192,256]{1,0:T(8,128)(2,1)S(1)} %get-tuple-element.8.lr, f32[128,256]{1,0:T(8,128)S(1)} %get-tuple-element.9.wt, f32[128,256]{1,0:T(8,128)S(1)} %get-tuple-element.10.bt), custom_call_target="tpu_custom_call" | custom-call | tf_op jit(solution)/shard_map/finish/pallas_call | solution.py:514

commit v5 on v4

--- a/solution.py
+++ b/solution.py
@@ -191,7 +191,7 @@
     pump(PUMP1)
 
     load_e.wait()
-    base = min(512, width)
+    base = min(1024, width)
 
     @pl.loop(0, width // base)
     def _(i):
@@ -204,7 +204,7 @@
     gbhl[...] = split_columns(gb[c, x] + gbx[0] + gbx[1] + gbx[2])
 
     def partial(h, k):
-        tile = min(512, hc)
+        tile = min(1024, hc)
 
         @pl.loop(0, hc // tile)
         def _(i):
@@ -316,7 +316,7 @@
 
     def gather_core(k):
         da_copies[k].wait_recv()
-        tile = min(512, hc)
+        tile = min(1024, hc)
         for h in range(2):
             @pl.loop(0, hc // tile)
             def _(i):

time: 121 us -> 121 us (level)
  no operation moved by 1% of the time
where the time goes in v5:
time: 121 us; the launch traced here: 119 us
  Pallas kernels  118 us (98%)
    pallas_call x1, Pallas kernels, shards(): pl.pallas_call(functools.partial(exchange, nz, 1.0 / replicas), out_shape...  112 us
    pallas_call x1, Pallas kernels, shards(): pl.pallas_call(finish, out_shape=(jax.ShapeDtypeStruct((share, cols), bf1...  6.16 us

profile of v5, /device:TPU:2, one launch (start us, length us, event | category | flops | bytes accessed | tf_op | source)
XLA Modules:
  0.0 118.8 jit_solution(6765465397367406157)
XLA Ops:
  0.6 111.9 %exchange.1 = (f32[8192,256]{1,0:T(8,128)S(1)}, bf16[8192,256]{1,0:T(8,128)(2,1)S(1)}, f32[128,256]{1,0:T(8,128)S(1)}, f32[128,256]{1,0:T(8,128)S(1)}) custom-call(bf16[128,8192]{1,0:T(8,128)(2,1)} %x_hbm.1, bf16[1024,256]{1,0:T(8,128)(2,1)} %g_hbm.1, bf16[8192,256]{1,0:T(8,128)(2,1)} %bitcast.1, f32[256,128]{1,0:T(8,128)} %basis.1), custom_call_target="tpu_custom_call" | custom-call | tf_op jit(solution)/shard_map/exchange/pallas_call | solution.py:497
  112.5 6.2 %finish.1 = (bf16[256,256]{1,0:T(8,128)(2,1)}, bf16[1,8192,256]{2,1,0:T(8,128)(2,1)}, f32[256,128]{1,0:T(8,128)}) custom-call(f32[8192,256]{1,0:T(8,128)S(1)} %get-tuple-element.7.merged, bf16[8192,256]{1,0:T(8,128)(2,1)S(1)} %get-tuple-element.8.lr, f32[128,256]{1,0:T(8,128)S(1)} %get-tuple-element.9.wt, f32[128,256]{1,0:T(8,128)S(1)} %get-tuple-element.10.bt), custom_call_target="tpu_custom_call" | custom-call | tf_op jit(solution)/shard_map/finish/pallas_call | solution.py:514
